TPU v7x, 32 devices: a whole 2x2x4 slice. The times are simulated.
32 devices in a mesh: req: 8 (over y, x, core), tp: 4 (over z).
Axes of the slice: x: 2, y: 2, z: 4, core: 2. Of those that a mesh axis runs over, the one named last changes fastest.
Arguments:
- embeds: bfloat16 [2048, 2048], P(('req', 'tp')), may hold values from -25 to 25
- input_norm_gain: float32 [2048], replicated, may hold values from 0.25 to 1.75
- input_norm_bias: float32 [2048], replicated, may hold values from -3 to 3
- joined_projection_weight: bfloat16 [2048, 6144], P(None, 'tp'), may hold values from -0.125 to 0.125
- joined_projection_bias: float32 [6144], P('tp'), may hold values from -3 to 3
- adapter_down_weight: bfloat16 [4, 2048, 16], replicated, may hold values from -0.125 to 0.125
- adapter_up_weight: bfloat16 [4, 16, 6144], P(None, None, 'tp'), may hold values from -1.5 to 1.5
- attention_out_weight: bfloat16 [2048, 2048], P('tp'), may hold values from -0.125 to 0.125
- attention_out_bias: float32 [2048], replicated, may hold values from -3 to 3
- post_attention_norm_gain: float32 [2048], replicated, may hold values from 0.4 to 1.6
- post_attention_norm_bias: float32 [2048], replicated, may hold values from -3 to 3
- feedforward_up_weight: bfloat16 [2048, 4096], P(None, 'tp'), may hold values from -0.125 to 0.125
- feedforward_up_bias: float32 [4096], P('tp'), may hold values from -3 to 3
- feedforward_down_weight: bfloat16 [4096, 2048], P('tp'), may hold values from -0.09375 to 0.09375
- feedforward_down_bias: float32 [2048], replicated, may hold values from -3 to 3
- stored_keys: bfloat16 [8, 1024, 2048], P('req', None, 'tp'), may hold values from -400 to 400
- stored_values: bfloat16 [8, 1024, 2048], P('req', None, 'tp'), may hold values from -6 to 6
- stored_length: int32 [8], P('req'), may hold values from 2 to 1024, as said below
- tenant_first_request: int32 [3], replicated, may hold values from 1 to 7, as said below
- accept: int32 [2048], P(('req', 'tp')), may hold values 0 or 1
- replacement_token_index: int32 [2048], P('req'), may hold values from 0 to 50175, as said below
- word_embedding_table: bfloat16 [50176, 2048], P('req', 'tp'), may hold values from -6 to 6
Outputs:
- denoised: bfloat16 [2048, 2048], P(('req', 'tp'))
Inputs may be any that keep to these rules, and one draw needn't show every extreme that they name: `stored_length`: one request has exactly 1024 cached positions. `tenant_first_request`: strictly increasing. `replacement_token_index`: of the 256 ids of one index of req, at most 96 lie in the rows o * 6272 to (o + 1) * 6272 - 1 of any one index o of req; one index o receives exactly 96 from every index of req, and every other index receives about equally many.
All inputs are finite; a program needn't handle non-finite values. No bound on the sum of `accept` on one device may be relied on, other than what follows from the above.
Results may differ from a plain program's by a relative error of at most 0.04.
Values may be sent and summed in bfloat16 or wider, within the bound.
A program may use at most 128 MiB of HBM per device.

v0:
```python
import jax
import jax.numpy as jnp
from jax import lax
from jax.sharding import PartitionSpec as P

H = 16
HD = 128
BLK = 256
EPSILON = 1e-05


def layer_norm(residual_state, gain, shift):
    values = residual_state.astype(jnp.float32)
    row_mean = jnp.mean(values, axis=-1, keepdims=True)
    centered = values - row_mean
    variance = jnp.mean(centered * centered, axis=-1, keepdims=True)
    return (centered * lax.rsqrt(variance + EPSILON) * gain + shift).astype(jnp.bfloat16)


def attend(queries, keys_block, values_block, keys_cache, values_cache, length, slopes):
    block_len = queries.shape[0]
    local_heads = queries.shape[1]
    head_size = queries.shape[2]
    score_scale = 1.0 / jnp.sqrt(jnp.float32(head_size))
    block_pos = jnp.arange(block_len)
    query_pos = length + block_pos
    scores = (
        jnp.einsum("qhd,khd->hqk", queries, keys_block, preferred_element_type=jnp.float32)
        * score_scale
    )
    distance = jnp.abs(block_pos[:, None] - block_pos[None, :]).astype(jnp.float32)
    scores = scores - slopes[:, None, None] * distance[None, :, :]
    row_max = jnp.max(scores, axis=-1)
    weights = jnp.exp(scores - row_max[..., None])
    row_total = jnp.sum(weights, axis=-1)
    accum = jnp.einsum(
        "hqk,khd->hqd",
        weights.astype(jnp.bfloat16),
        values_block,
        preferred_element_type=jnp.float32,
    )
    cache_rows = keys_cache.shape[0]
    tile_len = min(512, cache_rows)
    tile_count = (length + tile_len - 1) // tile_len

    def cache_step(index, state_in):
        old_max, old_total, old_accum = state_in
        first_pos = index * tile_len
        key_tile = lax.dynamic_slice_in_dim(keys_cache, first_pos, tile_len, 0).reshape(
            tile_len, local_heads, head_size
        )
        value_tile = lax.dynamic_slice_in_dim(values_cache, first_pos, tile_len, 0).reshape(
            tile_len, local_heads, head_size
        )
        key_pos = first_pos + jnp.arange(tile_len)
        tile_scores = (
            jnp.einsum("qhd,khd->hqk", queries, key_tile, preferred_element_type=jnp.float32)
            * score_scale
        )
        gaps = (query_pos[:, None] - key_pos[None, :]).astype(jnp.float32)
        tile_scores = tile_scores - slopes[:, None, None] * gaps[None, :, :]
        tile_scores = jnp.where((key_pos < length)[None, None, :], tile_scores, -jnp.inf)
        new_max = jnp.maximum(old_max, jnp.max(tile_scores, axis=-1))
        shrink = jnp.exp(old_max - new_max)
        tile_weights = jnp.exp(tile_scores - new_max[..., None])
        new_total = old_total * shrink + jnp.sum(tile_weights, axis=-1)
        new_accum = old_accum * shrink[..., None] + jnp.einsum(
            "hqk,khd->hqd",
            tile_weights.astype(jnp.bfloat16),
            value_tile,
            preferred_element_type=jnp.float32,
        )
        return (new_max, new_total, new_accum)

    row_max, row_total, accum = lax.fori_loop(
        0, tile_count, cache_step, (row_max, row_total, accum)
    )
    context = (accum / row_total[..., None]).astype(jnp.bfloat16)
    return jnp.transpose(context, (1, 0, 2)).reshape(block_len, local_heads * head_size)


def shards(
    embeds,
    input_norm_gain,
    input_norm_bias,
    joined_projection_weight,
    joined_projection_bias,
    adapter_down_weight,
    adapter_up_weight,
    attention_out_weight,
    attention_out_bias,
    post_attention_norm_gain,
    post_attention_norm_bias,
    feedforward_up_weight,
    feedforward_up_bias,
    feedforward_down_weight,
    feedforward_down_bias,
    stored_keys,
    stored_values,
    stored_length,
    tenant_first_request,
    accept,
    replacement_token_index,
    word_embedding_table,
):
    tp_rank = lax.axis_index("tp")
    req_rank = lax.axis_index("req")
    local_heads = joined_projection_weight.shape[1] // (3 * HD)
    requests = stored_keys.shape[0]
    tok_rows = requests * BLK
    share_rows = embeds.shape[0]
    table_rows = word_embedding_table.shape[0]
    head_index = tp_rank * local_heads + jnp.arange(local_heads)
    slopes = jnp.exp2(-8.0 * (head_index + 1).astype(jnp.float32) / H)
    owned = req_rank * requests + jnp.arange(requests)
    tenant_index = jnp.sum(
        (owned[:, None] >= tenant_first_request[None, :]).astype(jnp.int32), axis=1
    )
    adapter_inputs = [
        lax.dynamic_index_in_dim(adapter_down_weight, tenant_index[0], 0, keepdims=False)
    ]
    adapter_outputs = [
        lax.dynamic_index_in_dim(adapter_up_weight, tenant_index[0], 0, keepdims=False)
    ]

    def project(shard_rows):
        joined = jnp.dot(shard_rows, joined_projection_weight, preferred_element_type=jnp.float32)
        row_request = jnp.arange(shard_rows.shape[0]) // BLK
        low_rank_rows = jnp.dot(
            shard_rows, adapter_inputs[0], preferred_element_type=jnp.float32
        ).astype(jnp.bfloat16)
        lifted = jnp.dot(low_rank_rows, adapter_outputs[0], preferred_element_type=jnp.float32)
        joined = joined + jnp.where((row_request == 0)[:, None], lifted, 0.0)
        return (joined + joined_projection_bias).astype(jnp.bfloat16)

    def expand(shard_rows):
        inner = (
            jnp.dot(shard_rows, feedforward_up_weight, preferred_element_type=jnp.float32)
            + feedforward_up_bias
        )
        return jax.nn.gelu(inner, approximate=True).astype(jnp.bfloat16)

    def share_sum(left, right):
        partial_sum = jnp.dot(left, right, preferred_element_type=jnp.float32)
        summed = lax.psum(partial_sum.astype(jnp.bfloat16), "tp").astype(jnp.float32)
        return lax.dynamic_slice_in_dim(summed, tp_rank * share_rows, share_rows, 0)

    def run_layer_pass(residual_state):
        normed = layer_norm(residual_state, input_norm_gain, input_norm_bias)
        joined = project(lax.all_gather(normed, "tp", axis=0, tiled=True))
        heads_view = joined.reshape(tok_rows, local_heads, 3, HD)
        contexts = attend(
            heads_view[:, :, 0],
            heads_view[:, :, 1],
            heads_view[:, :, 2],
            stored_keys[0],
            stored_values[0],
            stored_length[0],
            slopes,
        )
        attended = (
            residual_state.astype(jnp.float32)
            + share_sum(contexts, attention_out_weight)
            + attention_out_bias
        ).astype(jnp.bfloat16)
        post = layer_norm(attended, post_attention_norm_gain, post_attention_norm_bias)
        hidden = expand(lax.all_gather(post, "tp", axis=0, tiled=True))
        return (
            attended.astype(jnp.float32)
            + share_sum(hidden, feedforward_down_weight)
            + feedforward_down_bias
        ).astype(jnp.bfloat16)

    all_ids = lax.all_gather(replacement_token_index, "req", axis=0, tiled=True)
    local_index = all_ids - req_rank * table_rows
    inside = (local_index >= 0) & (local_index < table_rows)
    found = jnp.take(word_embedding_table, jnp.clip(local_index, 0, table_rows - 1), axis=0)
    columns = lax.psum_scatter(
        jnp.where(inside[:, None], found.astype(jnp.float32), 0.0).astype(jnp.bfloat16),
        "req",
        scatter_dimension=0,
        tiled=True,
    )
    replacement = lax.all_to_all(columns, "tp", split_axis=0, concat_axis=1, tiled=True)
    first = run_layer_pass(embeds)
    second_in = jnp.where((accept == 1)[:, None], replacement, first)
    return run_layer_pass(second_in)


def solution(mesh):
    in_specs = (
        P(("req", "tp"), None),
        P(),
        P(),
        P(None, "tp"),
        P("tp"),
        P(),
        P(None, None, "tp"),
        P("tp", None),
        P(),
        P(),
        P(),
        P(None, "tp"),
        P("tp"),
        P("tp", None),
        P(),
        P("req", None, "tp"),
        P("req", None, "tp"),
        P("req"),
        P(),
        P(("req", "tp")),
        P("req"),
        P("req", "tp"),
    )
    out_specs = P(("req", "tp"), None)
    return jax.shard_map(shards, mesh=mesh, in_specs=in_specs, out_specs=out_specs, check_vma=False)
```

profile of v0, /device:TPU:0, one launch (start us, length us, event | category | flops | bytes accessed | tf_op | source)
XLA Modules:
  0.0 432.1 jit_solution(809088786829762818)
XLA Ops:
  7.4 1.2 convert_reduce_fusion.3
  8.6 1.2 fusion.64
  9.8 1.8 fusion.67
  12.4 1.3 fusion.113
  15.0 1.5 copy.67
  16.5 2.3 copy.68
  19.5 23.0 %all-gather.6.cloned.1.call-done = bf16[256,2048]{1,0:T(8,128)(2,1)} async-done(((bf16[64,2048]{1,0:T(8,128)(2,1)}), bf16[256,2048]{1,0:T(8,128)(2,1)}) %all-gather.6.cloned.1.call-update) | async-done | bytes 1048592 | tf_op jit(solution)/shard_map/all_gather | solution.py:150
  42.5 6.1 %fusion.131 = f32[256,1536]{1,0:T(8,128)} fusion(bf16[256,2048]{1,0:T(8,128)(2,1)} %all-gather.6.cloned.1.call-done, bf16[2048,1536]{1,0:T(8,128)(2,1)} %param.29), kind=kOutput, calls=%fused_computation.196 | convolution fusion | flops 1610612736 | bytes 8912896 | tf_op jit(solution)/shard_map/dot_general | solution.py:127
  48.6 3.8 fusion.23
  52.4 2.3 copy.62
  54.7 1.4 fusion.129
  56.1 2.1 fusion.78
  58.4 1.0 slice.26
  60.2 5.2 %while.32 = (s32[]{:T(128)}, f32[4,256]{1,0:T(4,128)S(1)}, f32[4,256]{1,0:T(4,128)S(1)}, f32[4,256,128]{2,1,0:T(8,128)}, s32[]{:T(128)}, /*index=5*/s32[]{:T(128...) while((s32[]{:T(128)}, f32[4,256]{1,0:T(4,128)S(1)}, ...), condition=%wide.region_9.10_spmd.clone.clone, body=%wide.region_6.9_spmd.clone.clone.sunk | while | flops 273682176 | bytes 17112384 | solution.py:75
  60.2 1.2 constant_dynamic-slice_fusion.6
  65.3 2.1 copy.69
  67.4 1.1 divide_convert_fusion.1
  68.5 1.8 convolution_convert_fusion.1
  70.4 55.7 %all-reduce.5.cloned.1.call-done = bf16[256,2048]{1,0:T(8,128)(2,1)} async-done(((bf16[256,2048]{1,0:T(8,128)(2,1)}), bf16[256,2048]{1,0:T(8,128)(2,1)}) %all-reduce.5.cloned.1.call-update) | async-done | bytes 1048592 | tf_op jit(solution)/shard_map/psum | solution.py:145
  126.1 1.1 convert_reduce_fusion.2
  128.9 8.9 %all-gather = s32[8,1,256]{2,1,0:T(1,128)S(1)} all-gather(s32[1,1,256]{2,1,0:T(1,128)S(1)} %bitcast.137), channel_id=1, replica_groups=mesh['req'=8,'tp'=4] {'req'}, dimensions={0}, use_global_device_ids=true | all-gather | bytes 9216 | tf_op jit(solution)/shard_map/all_gather | solution.py:174
  137.8 12.9 %gather_fusion = bf16[2048,512]{1,0:T(8,128)(2,1)} fusion(bf16[6272,512]{1,0:T(8,128)(2,1)} %param.47, s32[2048]{0:T(1024)S(1)} %fusion.107), kind=kCustom, calls=%fused_computation | custom fusion | bytes 4202496 | tf_op jit(solution)/shard_map/jit(_take)/gather | solution.py:177
  150.7 3.0 select_convert_fusion
  153.8 2.5 all-gather.8.cloned.1.call-done
  156.3 7.7 %convolution_convert_fusion.3 = bf16[256,2048]{1,0:T(8,128)(2,1)} fusion(bf16[1024,2048]{1,0:T(8,128)(2,1)} %param.39, bf16[256,2048]{1,0:T(8,128)(2,1)} %all-gather.8.cloned.1.call-done, bf16[2048,1024]{1,0:T(8,128)(2,1)} %param.37, f32[1024]{0:T(1024)S(1)} %copy-done.18), kind=kOutput, calls=%fused_computation.49 | convolution fusion | flops 2150629376 | bytes 10489856 | tf_op jit(solution)/shard_map/dot_general | solution.py:144
  164.0 29.5 %reduce-scatter.2.cloned.1.call-done = bf16[256,512]{1,0:T(8,128)(2,1)} async-done(((bf16[2048,512]{1,0:T(8,128)(2,1)}), bf16[256,512]{1,0:T(8,128)(2,1)}) %reduce-scatter.2.cloned.1.call-update) | async-done | bytes 262160 | tf_op jit(solution)/shard_map/reduce_scatter | solution.py:178
  193.5 4.6 %all-to-all-start = ((bf16[4,64,512]{2,1,0:T(8,128)(2,1)}), bf16[4,64,512]{2,1,0:T(8,128)(2,1)S(1)}, u32[]{:S(2)}, u32[]{:S(2)}) async-start(bf16[4,64,512]{2,1,0:T(8,128)(2,1)} %bitcast.134), calls=%async_computation.1 | async-start | bytes 524288 | tf_op jit(solution)/shard_map/all_to_all | solution.py:184
  198.1 16.4 %all-to-all-done = bf16[4,64,512]{2,1,0:T(8,128)(2,1)S(1)} async-done(((bf16[4,64,512]{2,1,0:T(8,128)(2,1)}), bf16[4,64,512]{2,1,0:T(8,128)(2,1)S(1)}, u32[]{:S(2)}, u32[]{:S(2)}) %all-to-all-start) | async-done | bytes 262176 | tf_op jit(solution)/shard_map/all_to_all | solution.py:184
  215.2 6.2 %all-reduce.7.cloned.1.call-done = bf16[256,2048]{1,0:T(8,128)(2,1)} async-done(((bf16[256,2048]{1,0:T(8,128)(2,1)}), bf16[256,2048]{1,0:T(8,128)(2,1)}) %all-reduce.7.cloned.1.call-update) | async-done | bytes 1048592 | tf_op jit(solution)/shard_map/psum | solution.py:145
  221.5 1.4 convert_reduce_fusion.1
  224.0 26.8 %all-gather.10.cloned.1.call-done = bf16[256,2048]{1,0:T(8,128)(2,1)} async-done(((bf16[64,2048]{1,0:T(8,128)(2,1)}), bf16[256,2048]{1,0:T(8,128)(2,1)}) %all-gather.10.cloned.1.call-update) | async-done | bytes 1048592 | tf_op jit(solution)/shard_map/all_gather | solution.py:150
  250.9 6.1 %fusion.132 = f32[256,1536]{1,0:T(8,128)} fusion(bf16[256,2048]{1,0:T(8,128)(2,1)} %all-gather.10.cloned.1.call-done, bf16[2048,1536]{1,0:T(8,128)(2,1)} %param.29), kind=kOutput, calls=%fused_computation.197 | convolution fusion | flops 1610612736 | bytes 8912896 | tf_op jit(solution)/shard_map/dot_general | solution.py:127
  256.9 3.8 fusion.22
  260.8 2.3 copy.70
  263.0 1.5 fusion.130
  264.5 2.1 fusion.76
  266.8 1.7 slice.29
  268.5 1.8 copy.87
  270.3 5.2 %while.33 = (s32[]{:T(128)}, f32[4,256]{1,0:T(4,128)S(1)}, f32[4,256]{1,0:T(4,128)S(1)}, f32[4,256,128]{2,1,0:T(8,128)}, s32[]{:T(128)}, /*index=5*/s32[]{:T(128...) while((s32[]{:T(128)}, f32[4,256]{1,0:T(4,128)S(1)}, ...), condition=%wide.region_21.22_spmd.clone.clone, body=%wide.region_18.21_spmd.clone.clone.sunk | while | flops 273682176 | bytes 17112384 | solution.py:75
  270.3 1.2 constant_dynamic-slice_fusion.7
  275.4 1.2 copy.75
  276.7 1.8 convolution_convert_fusion
  278.6 55.7 %all-reduce.9.cloned.1.call-done = bf16[256,2048]{1,0:T(8,128)(2,1)} async-done(((bf16[256,2048]{1,0:T(8,128)(2,1)}), bf16[256,2048]{1,0:T(8,128)(2,1)}) %all-reduce.9.cloned.1.call-update) | async-done | bytes 1048592 | tf_op jit(solution)/shard_map/psum | solution.py:145
  334.2 1.1 convert_reduce_fusion
  336.6 27.4 %all-gather.12.cloned.1.call-done = bf16[256,2048]{1,0:T(8,128)(2,1)} async-done(((bf16[64,2048]{1,0:T(8,128)(2,1)}), bf16[256,2048]{1,0:T(8,128)(2,1)}) %all-gather.12.cloned.1.call-update) | async-done | bytes 1048592 | tf_op jit(solution)/shard_map/all_gather | solution.py:167
  364.0 7.4 %convolution_convert_fusion.2 = bf16[256,2048]{1,0:T(8,128)(2,1)} fusion(bf16[1024,2048]{1,0:T(8,128)(2,1)} %param.39, bf16[256,2048]{1,0:T(8,128)(2,1)} %all-gather.12.cloned.1.call-done, bf16[2048,1024]{1,0:T(8,128)(2,1)} %param.37, f32[1024]{0:T(1024)S(1)} %copy-done.18), kind=kOutput, calls=%fused_computation.48 | convolution fusion | flops 2150629376 | bytes 10489856 | tf_op jit(solution)/shard_map/dot_general | solution.py:144
  371.4 51.5 %all-reduce.11.cloned.1.call-done = bf16[256,2048]{1,0:T(8,128)(2,1)} async-done(((bf16[256,2048]{1,0:T(8,128)(2,1)}), bf16[256,2048]{1,0:T(8,128)(2,1)}) %all-reduce.11.cloned.1.call-update) | async-done | bytes 1048592 | tf_op jit(solution)/shard_map/psum | solution.py:145
  422.9 1.7 fusion.75
  (108 shorter events, 14.2 us)
Async XLA Ops:
  7.4 61.1 %copy-start = (bf16[512,2048]{1,0:T(8,128)(2,1)S(1)}, bf16[512,2048]{1,0:T(8,128)(2,1)}, u32[]{:S(2)}) copy-start(bf16[512,2048]{1,0:T(8,128)(2,1)} %param.33) | copy-start | bytes 6291460
  7.4 35.1 %all-gather.6.cloned.1.call-start = ((), (), s32[]{:S(2)}) async-start(), calls=%async_computation.3 | async-start | bytes 1310720 | tf_op jit(solution)/shard_map/all_gather | solution.py:150
  11.7 114.4 %all-reduce.5.cloned.1.call-start = ((), (), s32[]{:S(2)}) async-start(), calls=%async_computation.4 | async-start | bytes 2097152 | tf_op jit(solution)/shard_map/psum | solution.py:145
  19.5 35.2 %copy-start.7 = (f32[256,256]{0,1:T(8,128)}, f32[256,256]{0,1:T(8,128)S(1)}, u32[]{:S(2)}) copy-start(f32[256,256]{0,1:T(8,128)S(1)} %abs_convert_fusion) | copy-start | bytes 786436
  19.5 29.0 %copy-start.12 = (f32[1536]{0:T(1024)S(1)}, f32[1536]{0:T(1024)}, u32[]{:S(2)}) copy-start(f32[1536]{0:T(1024)} %param.30) | copy-start | bytes 18436
  60.2 2.7 copy-start.9
  62.8 1.0 copy-start.1
  64.5 0.8 copy-start.2
  68.5 57.6 %copy-start.6 = (bf16[64,2048]{1,0:T(8,128)(2,1)S(1)}, bf16[64,2048]{1,0:T(8,128)(2,1)}, u32[]{:S(2)}) copy-start(bf16[64,2048]{1,0:T(8,128)(2,1)} %param.26) | copy-start | bytes 786436
  68.5 57.6 %copy-start.13 = (f32[2048]{0:T(1024)S(1)}, f32[2048]{0:T(1024)}, u32[]{:S(2)}) copy-start(f32[2048]{0:T(1024)} %param.34) | copy-start | bytes 24580
  68.5 59.4 %copy-start.14 = (f32[2048]{0:T(1024)S(1)}, f32[2048]{0:T(1024)}, u32[]{:S(2)}) copy-start(f32[2048]{0:T(1024)} %param.36) | copy-start | bytes 24580
  68.5 59.4 %copy-start.15 = (f32[2048]{0:T(1024)S(1)}, f32[2048]{0:T(1024)}, u32[]{:S(2)}) copy-start(f32[2048]{0:T(1024)} %param.35) | copy-start | bytes 24580
  70.3 58.6 %copy-start.17 = (s32[256]{0:T(256)S(1)}, s32[256]{0:T(256)}, u32[]{:S(2)}) copy-start(s32[256]{0:T(256)} %param.46) | copy-start | bytes 3076
  70.3 86.0 %all-gather.8.cloned.1.call-start = ((), (), s32[]{:S(2)}) async-start(), calls=%async_computation.5 | async-start | bytes 1310720 | tf_op jit(solution)/shard_map/all_gather | solution.py:167
  127.2 0.7 copy-start.5
  128.8 64.7 %reduce-scatter.2.cloned.1.call-start = ((), (), s32[]{:S(2)}) async-start(), calls=%async_computation.2 | async-start | bytes 2359296 | tf_op jit(solution)/shard_map/reduce_scatter | solution.py:178
  153.7 2.6 copy-start.18
  153.7 44.4 %copy-start.19 = (s32[64]{0:T(128)S(1)}, s32[64]{0:T(128)}, u32[]{:S(2)}) copy-start(s32[64]{0:T(128)} %param.45) | copy-start | bytes 772
  153.7 67.7 %all-reduce.7.cloned.1.call-start = ((), (), s32[]{:S(2)}) async-start(), calls=%async_computation.6 | async-start | bytes 2097152 | tf_op jit(solution)/shard_map/psum | solution.py:145
  164.0 57.5 %copy-start.16 = (f32[2048]{0:T(1024)S(1)}, f32[2048]{0:T(1024)}, u32[]{:S(2)}) copy-start(f32[2048]{0:T(1024)} %param.40) | copy-start | bytes 24580
  164.0 59.1 %copy-start.10 = (f32[2048]{0:T(1024)S(1)}, f32[2048]{0:T(1024)}, u32[]{:S(2)}) copy-start(f32[2048]{0:T(1024)} %param.28) | copy-start | bytes 24580
  164.0 59.1 %copy-start.11 = (f32[2048]{0:T(1024)S(1)}, f32[2048]{0:T(1024)}, u32[]{:S(2)}) copy-start(f32[2048]{0:T(1024)} %param.27) | copy-start | bytes 24580
  193.5 21.0 %all-to-all-start = ((bf16[4,64,512]{2,1,0:T(8,128)(2,1)}), bf16[4,64,512]{2,1,0:T(8,128)(2,1)S(1)}, u32[]{:S(2)}, u32[]{:S(2)}) async-start(bf16[4,64,512]{2,1,0:T(8,128)(2,1)} %bitcast.134), calls=%async_computation.1 | async-start | bytes 524288 | tf_op jit(solution)/shard_map/all_to_all | solution.py:184
  198.1 52.8 %all-gather.10.cloned.1.call-start = ((), (), s32[]{:S(2)}) async-start(), calls=%async_computation.7 | async-start | bytes 1310720 | tf_op jit(solution)/shard_map/all_gather | solution.py:150
  224.0 110.3 %all-reduce.9.cloned.1.call-start = ((), (), s32[]{:S(2)}) async-start(), calls=%async_computation.8 | async-start | bytes 2097152 | tf_op jit(solution)/shard_map/psum | solution.py:145
  270.3 2.7 copy-start.8
  272.9 1.0 copy-start.3
  274.6 0.8 copy-start.4
  278.5 85.5 %all-gather.12.cloned.1.call-start = ((), (), s32[]{:S(2)}) async-start(), calls=%async_computation.9 | async-start | bytes 1310720 | tf_op jit(solution)/shard_map/all_gather | solution.py:167
  336.6 86.3 %all-reduce.11.cloned.1.call-start = ((), (), s32[]{:S(2)}) async-start(), calls=%async_computation.10 | async-start | bytes 2097152 | tf_op jit(solution)/shard_map/psum | solution.py:145
Sparse Core Ops, SparseCore 0:
  11.8 30.6 all-gather.5
  70.4 55.5 all-reduce.4
  128.9 27.3 all-gather.7
  164.1 57.2 all-reduce.6
  224.1 26.7 all-gather.9
  278.6 55.5 all-reduce.8
  336.7 27.3 all-gather.11
  371.5 51.3 all-reduce.10
Sparse Core Ops, SparseCore 1:
  153.8 39.7 reduce-scatter.1
where the time goes:
time: 433 us; the launch traced here: 432 us
  waiting for transfers between devices  295 us (68%)
  matrix products  48.1 us (11%)
  local copies, waits for them, and re-layouts  35 us (8%)
  other arithmetic  22.4 us (5%)
  between operations  17.8 us (4%)
  blocking collectives  8.86 us (2%)
  starting transfers between devices  4.9 us (1%)
    psum x4, waiting for transfers between devices, share_sum(): lax.psum(partial_sum.astype(jnp.bfloat16), 'tp').astype(jnp.float32)  169 us
    all_gather x2, waiting for transfers between devices, run_layer_pass(): joined = project(lax.all_gather(normed, 'tp', axis=0, tiled=True))  49.8 us
    all_gather x2, waiting for transfers between devices, run_layer_pass(): hidden = expand(lax.all_gather(post, 'tp', axis=0, tiled=True))  29.9 us
    reduce_scatter x1, waiting for transfers between devices, shards(): lax.psum_scatter(jnp.where(inside[:, None], found.astype(jnp.float32), 0....  29.5 us
    dot_general x4, matrix products, share_sum(): partial_sum = jnp.dot(left, right, preferred_element_type=jnp.float32)  18.6 us
    all_to_all x1, waiting for transfers between devices, shards(): lax.all_to_all(columns, 'tp', split_axis=0, concat_axis=1, tiled=True)  16.4 us
    gather x1, local copies, waits for them, and re-layouts, shards(): jnp.take(word_embedding_table, jnp.clip(local_index, 0, table_rows - 1),...  12.9 us
    dot_general x2, matrix products, project(): jnp.dot(shard_rows, joined_projection_weight, preferred_element_type=jnp....  12.1 us
  transfers between devices with their start and end apart: 10, of which 10 were waited for; matrix products, arithmetic and copies ran while one was open for 7% of the time, Pallas kernels for 0%

commit v1 on v0

--- a/solution.py
+++ b/solution.py
@@ -7,6 +7,18 @@
 HD = 128
 BLK = 256
 EPSILON = 1e-05
+
+
+def collect(array, axis, dim):
+    ways, here, step = (lax.axis_size(axis), lax.axis_index(axis), array.shape[dim])
+    line, have = (array, 1)
+    while have < ways:
+        line = jnp.concatenate(
+            [line, lax.ppermute(line, axis, [(d, (d - have) % ways) for d in range(ways)])],
+            axis=dim,
+        )
+        have = 2 * have
+    return jnp.roll(line, here * step, axis=dim)
 
 
 def layer_norm(residual_state, gain, shift):
@@ -147,7 +159,7 @@
 
     def run_layer_pass(residual_state):
         normed = layer_norm(residual_state, input_norm_gain, input_norm_bias)
-        joined = project(lax.all_gather(normed, "tp", axis=0, tiled=True))
+        joined = project(collect(normed, "tp", 0))
         heads_view = joined.reshape(tok_rows, local_heads, 3, HD)
         contexts = attend(
             heads_view[:, :, 0],

time: 433 us -> 453 us (1.046)
  other arithmetic: 22.4 us -> 30.7 us
  starting transfers between devices: 4.9 us -> 12.6 us
    ppermute x0 -> x4, waiting for transfers between devices: none -> 54.3 us  [collect(): lax.ppermute(line, axis, [(d, (d - have) % ways) for d in range(ways)])]
    all_gather x2 -> x0, waiting for transfers between devices: 49.8 us -> none  [run_layer_pass(): joined = project(lax.all_gather(normed, 'tp', axis=0, tiled=True))]
    concatenate x0 -> x4, other arithmetic: none -> 9.64 us  [the longest x2 7.82 us: collect(): return jnp.roll(line, here * step, axis=dim)]
    ppermute x0 -> x4, starting transfers between devices: none -> 7.61 us  [collect(): lax.ppermute(line, axis, [(d, (d - have) % ways) for d in range(ways)])]
  transfers between devices with their start and end apart: 10 -> 12, of which waited for: 10 -> 12; matrix products, arithmetic and copies ran while one was open for 7% -> 7% of each run, Pallas kernels for 0% -> 0%
where the time goes in v1:
time: 453 us; the launch traced here: 452 us
  waiting for transfers between devices  299 us (66%)
  matrix products  47.9 us (11%)
  local copies, waits for them, and re-layouts  35 us (8%)
  other arithmetic  30.7 us (7%)
  between operations  17.8 us (4%)
  starting transfers between devices  12.6 us (3%)
  blocking collectives  8.86 us (2%)
    psum x4, waiting for transfers between devices, share_sum(): lax.psum(partial_sum.astype(jnp.bfloat16), 'tp').astype(jnp.float32)  169 us
    ppermute x4, waiting for transfers between devices, collect(): lax.ppermute(line, axis, [(d, (d - have) % ways) for d in range(ways)])  54.3 us
    all_gather x2, waiting for transfers between devices, run_layer_pass(): hidden = expand(lax.all_gather(post, 'tp', axis=0, tiled=True))  29.8 us
    reduce_scatter x1, waiting for transfers between devices, shards(): lax.psum_scatter(jnp.where(inside[:, None], found.astype(jnp.float32), 0....  29.5 us
    dot_general x4, matrix products, share_sum(): partial_sum = jnp.dot(left, right, preferred_element_type=jnp.float32)  18.6 us
    all_to_all x1, waiting for transfers between devices, shards(): lax.all_to_all(columns, 'tp', split_axis=0, concat_axis=1, tiled=True)  16.4 us
    gather x1, local copies, waits for them, and re-layouts, shards(): jnp.take(word_embedding_table, jnp.clip(local_index, 0, table_rows - 1),...  12.9 us
    dot_general x2, matrix products, project(): jnp.dot(shard_rows, joined_projection_weight, preferred_element_type=jnp....  12.4 us
  transfers between devices with their start and end apart: 12, of which 12 were waited for; matrix products, arithmetic and copies ran while one was open for 7% of the time, Pallas kernels for 0%

profile of v1, /device:TPU:0, one launch (start us, length us, event | category | flops | bytes accessed | tf_op | source)
XLA Modules:
  0.0 451.9 jit_solution(7376070617131104787)
XLA Ops:
  7.4 1.2 convert_reduce_fusion.3
  8.6 1.2 fusion.72
  11.0 5.1 %collective-permute-start = (bf16[64,2048]{1,0:T(8,128)(2,1)S(1)}, bf16[64,2048]{1,0:T(8,128)(2,1)S(1)}, u32[]{:S(2)}, u32[]{:S(2)}) collective-permute-start(bf16[64,2048]{1,0:T(8,128)(2,1)S(1)} %fusion.75), channel_id=1, source_target_pairs={{0,3},{1,0},{2,1},{3,2},{4,7},{5,4},{6,5},{7,6},{8,11},{9,8},{10,9... | collective-permute-start | bytes 786440 | tf_op jit(solution)/shard_map/ppermute | solution.py:17
  16.1 5.6 %collective-permute-done = bf16[64,2048]{1,0:T(8,128)(2,1)S(1)} collective-permute-done((bf16[64,2048]{1,0:T(8,128)(2,1)S(1)}, bf16[64,2048]{1,0:T(8,128)(2,1)S(1)}, u32[]{:S(2)}, u32[]{:S(2)}) %collective-permute-start) | collective-permute-done | bytes 262176 | tf_op jit(solution)/shard_map/ppermute | solution.py:17
  22.6 1.5 collective-permute-start.1
  26.7 1.5 copy.67
  28.2 2.3 copy.68
  31.9 15.9 %collective-permute-done.1 = bf16[128,2048]{1,0:T(8,128)(2,1)} collective-permute-done((bf16[128,2048]{1,0:T(8,128)(2,1)}, bf16[128,2048]{1,0:T(8,128)(2,1)}, u32[]{:S(2)}, u32[]{:S(2)}) %collective-permute-start.1) | collective-permute-done | bytes 524320 | tf_op jit(solution)/shard_map/ppermute | solution.py:17
  47.8 3.9 fusion.45
  51.7 3.6 convolution_select_fusion.1
  55.3 6.2 %fusion.20 = bf16[256,1536]{1,0:T(8,128)(2,1)} fusion(f32[256,1536]{1,0:T(8,128)} %convolution_select_fusion.1, bf16[256,2048]{1,0:T(8,128)(2,1)} %fusion.45, bf16[2048,1536]{1,0:T(8,128)(2,1)} %param.31, f32[1536]{0:T(1024)S(1)} %copy-done.20), kind=kOutput, calls=%fused_computation.48 | convolution fusion | flops 1611792384 | bytes 9705472 | tf_op jit(solution)/shard_map/dot_general | solution.py:139
  61.6 2.3 copy.62
  63.9 1.4 fusion.137
  65.2 2.1 fusion.86
  69.3 5.2 %while.32 = (s32[]{:T(128)}, f32[4,256]{1,0:T(4,128)S(1)}, f32[4,256]{1,0:T(4,128)S(1)}, f32[4,256,128]{2,1,0:T(8,128)}, s32[]{:T(128)}, /*index=5*/s32[]{:T(128...) while((s32[]{:T(128)}, f32[4,256]{1,0:T(4,128)S(1)}, ...), condition=%wide.region_9.11_spmd.clone.clone, body=%wide.region_6.10_spmd.clone.clone.sunk | while | flops 273682176 | bytes 17112384 | solution.py:87
  69.3 1.2 constant_dynamic-slice_fusion.6
  74.5 2.1 copy.69
  77.7 1.8 convolution_convert_fusion.1
  79.5 56.2 %all-reduce.5.cloned.1.call-done = bf16[256,2048]{1,0:T(8,128)(2,1)} async-done(((bf16[256,2048]{1,0:T(8,128)(2,1)}), bf16[256,2048]{1,0:T(8,128)(2,1)}) %all-reduce.5.cloned.1.call-update) | async-done | bytes 1048592 | tf_op jit(solution)/shard_map/psum | solution.py:157
  138.5 8.9 %all-gather = s32[8,1,256]{2,1,0:T(1,128)S(1)} all-gather(s32[1,1,256]{2,1,0:T(1,128)S(1)} %bitcast.137), channel_id=1, replica_groups=mesh['req'=8,'tp'=4] {'req'}, dimensions={0}, use_global_device_ids=true | all-gather | bytes 9216 | tf_op jit(solution)/shard_map/all_gather | solution.py:186
  147.5 12.9 %gather_fusion = bf16[2048,512]{1,0:T(8,128)(2,1)} fusion(bf16[6272,512]{1,0:T(8,128)(2,1)} %param.49, s32[2048]{0:T(1024)S(1)} %fusion.115), kind=kCustom, calls=%fused_computation | custom fusion | bytes 4202496 | tf_op jit(solution)/shard_map/jit(_take)/gather | solution.py:189
  160.3 3.0 select_convert_fusion
  163.6 2.3 all-gather.4.cloned.1.call-done
  165.9 7.7 %convolution_convert_fusion.3 = bf16[256,2048]{1,0:T(8,128)(2,1)} fusion(bf16[1024,2048]{1,0:T(8,128)(2,1)} %param.41, bf16[256,2048]{1,0:T(8,128)(2,1)} %all-gather.4.cloned.1.call-done, bf16[2048,1024]{1,0:T(8,128)(2,1)} %param.39, f32[1024]{0:T(1024)S(1)} %copy-done.21), kind=kOutput, calls=%fused_computation.47 | convolution fusion | flops 2150629376 | bytes 10489856 | tf_op jit(solution)/shard_map/dot_general | solution.py:156
  173.6 29.5 %reduce-scatter.2.cloned.1.call-done = bf16[256,512]{1,0:T(8,128)(2,1)} async-done(((bf16[2048,512]{1,0:T(8,128)(2,1)}), bf16[256,512]{1,0:T(8,128)(2,1)}) %reduce-scatter.2.cloned.1.call-update) | async-done | bytes 262160 | tf_op jit(solution)/shard_map/reduce_scatter | solution.py:190
  203.1 4.6 %all-to-all-start = ((bf16[4,64,512]{2,1,0:T(8,128)(2,1)}), bf16[4,64,512]{2,1,0:T(8,128)(2,1)S(1)}, u32[]{:S(2)}, u32[]{:S(2)}) async-start(bf16[4,64,512]{2,1,0:T(8,128)(2,1)} %bitcast.134), calls=%async_computation.1 | async-start | bytes 524288 | tf_op jit(solution)/shard_map/all_to_all | solution.py:196
  207.8 16.4 %all-to-all-done = bf16[4,64,512]{2,1,0:T(8,128)(2,1)S(1)} async-done(((bf16[4,64,512]{2,1,0:T(8,128)(2,1)}), bf16[4,64,512]{2,1,0:T(8,128)(2,1)S(1)}, u32[]{:S(2)}, u32[]{:S(2)}) %all-to-all-start) | async-done | bytes 262176 | tf_op jit(solution)/shard_map/all_to_all | solution.py:196
  224.9 6.2 %all-reduce.7.cloned.1.call-done = bf16[256,2048]{1,0:T(8,128)(2,1)} async-done(((bf16[256,2048]{1,0:T(8,128)(2,1)}), bf16[256,2048]{1,0:T(8,128)(2,1)}) %all-reduce.7.cloned.1.call-update) | async-done | bytes 1048592 | tf_op jit(solution)/shard_map/psum | solution.py:157
  231.1 1.4 convert_reduce_fusion.1
  234.0 7.3 %collective-permute-done.2 = bf16[64,2048]{1,0:T(8,128)(2,1)S(1)} collective-permute-done((bf16[64,2048]{1,0:T(8,128)(2,1)S(1)}, bf16[64,2048]{1,0:T(8,128)(2,1)S(1)}, u32[]{:S(2)}, u32[]{:S(2)}) %collective-permute-start.2) | collective-permute-done | bytes 262176 | tf_op jit(solution)/shard_map/ppermute | solution.py:17
  242.2 25.5 %collective-permute-done.3 = bf16[128,2048]{1,0:T(8,128)(2,1)} collective-permute-done((bf16[128,2048]{1,0:T(8,128)(2,1)}, bf16[128,2048]{1,0:T(8,128)(2,1)}, u32[]{:S(2)}, u32[]{:S(2)}) %collective-permute-start.3) | collective-permute-done | bytes 524320 | tf_op jit(solution)/shard_map/ppermute | solution.py:17
  267.7 3.9 fusion.40
  271.6 3.6 convolution_select_fusion
  275.2 6.2 %fusion.21 = bf16[256,1536]{1,0:T(8,128)(2,1)} fusion(f32[256,1536]{1,0:T(8,128)} %convolution_select_fusion, bf16[256,2048]{1,0:T(8,128)(2,1)} %fusion.40, bf16[2048,1536]{1,0:T(8,128)(2,1)} %param.31, f32[1536]{0:T(1024)S(1)} %copy-done.20), kind=kOutput, calls=%fused_computation.49 | convolution fusion | flops 1611792384 | bytes 9705472 | tf_op jit(solution)/shard_map/dot_general | solution.py:139
  281.3 2.3 copy.70
  283.6 1.5 fusion.138
  285.1 2.1 fusion.84
  287.4 1.7 slice.29
  289.1 1.8 copy.87
  290.8 5.2 %while.33 = (s32[]{:T(128)}, f32[4,256]{1,0:T(4,128)S(1)}, f32[4,256]{1,0:T(4,128)S(1)}, f32[4,256,128]{2,1,0:T(8,128)}, s32[]{:T(128)}, /*index=5*/s32[]{:T(128...) while((s32[]{:T(128)}, f32[4,256]{1,0:T(4,128)S(1)}, ...), condition=%wide.region_21.23_spmd.clone.clone, body=%wide.region_18.22_spmd.clone.clone.sunk | while | flops 273682176 | bytes 17112384 | solution.py:87
  290.8 1.2 constant_dynamic-slice_fusion.7
  296.0 1.2 copy.75
  297.3 1.8 convolution_convert_fusion
  299.1 55.0 %all-reduce.9.cloned.1.call-done = bf16[256,2048]{1,0:T(8,128)(2,1)} async-done(((bf16[256,2048]{1,0:T(8,128)(2,1)}), bf16[256,2048]{1,0:T(8,128)(2,1)}) %all-reduce.9.cloned.1.call-update) | async-done | bytes 1048592 | tf_op jit(solution)/shard_map/psum | solution.py:157
  356.5 27.4 %all-gather.6.cloned.1.call-done = bf16[256,2048]{1,0:T(8,128)(2,1)} async-done(((bf16[64,2048]{1,0:T(8,128)(2,1)}), bf16[256,2048]{1,0:T(8,128)(2,1)}) %all-gather.6.cloned.1.call-update) | async-done | bytes 1048592 | tf_op jit(solution)/shard_map/all_gather | solution.py:179
  383.9 7.3 %convolution_convert_fusion.2 = bf16[256,2048]{1,0:T(8,128)(2,1)} fusion(bf16[1024,2048]{1,0:T(8,128)(2,1)} %param.41, bf16[256,2048]{1,0:T(8,128)(2,1)} %all-gather.6.cloned.1.call-done, bf16[2048,1024]{1,0:T(8,128)(2,1)} %param.39, f32[1024]{0:T(1024)S(1)} %copy-done.21), kind=kOutput, calls=%fused_computation.46 | convolution fusion | flops 2150629376 | bytes 10489856 | tf_op jit(solution)/shard_map/dot_general | solution.py:156
  391.3 51.5 %all-reduce.11.cloned.1.call-done = bf16[256,2048]{1,0:T(8,128)(2,1)} async-done(((bf16[256,2048]{1,0:T(8,128)(2,1)}), bf16[256,2048]{1,0:T(8,128)(2,1)}) %all-reduce.11.cloned.1.call-update) | async-done | bytes 1048592 | tf_op jit(solution)/shard_map/psum | solution.py:157
  442.7 1.7 fusion.83
  (122 shorter events, 23.3 us)
Async XLA Ops:
  7.4 70.3 %copy-start = (bf16[512,2048]{1,0:T(8,128)(2,1)S(1)}, bf16[512,2048]{1,0:T(8,128)(2,1)}, u32[]{:S(2)}) copy-start(bf16[512,2048]{1,0:T(8,128)(2,1)} %param.35) | copy-start | bytes 6291460
  7.4 16.7 %copy-start.22 = (s32[3]{0:T(128)S(1)}, s32[3]{0:T(128)}, u32[]{:S(2)}) copy-start(s32[3]{0:T(128)} %param.46) | copy-start | bytes 40
  7.4 128.3 %all-reduce.5.cloned.1.call-start = ((), (), s32[]{:S(2)}) async-start(), calls=%async_computation.3 | async-start | bytes 2097152 | tf_op jit(solution)/shard_map/psum | solution.py:157
  11.0 10.7 %collective-permute-start = (bf16[64,2048]{1,0:T(8,128)(2,1)S(1)}, bf16[64,2048]{1,0:T(8,128)(2,1)S(1)}, u32[]{:S(2)}, u32[]{:S(2)}) collective-permute-start(bf16[64,2048]{1,0:T(8,128)(2,1)S(1)} %fusion.75), channel_id=1, source_target_pairs={{0,3},{1,0},{2,1},{3,2},{4,7},{5,4},{6,5},{7,6},{8,11},{9,8},{10,9... | collective-permute-start | bytes 786440 | tf_op jit(solution)/shard_map/ppermute | solution.py:17
  21.7 5.0 %copy-start.9 = (bf16[64,2048]{1,0:T(8,128)(2,1)}, bf16[64,2048]{1,0:T(8,128)(2,1)S(1)}, u32[]{:S(2)}) copy-start(bf16[64,2048]{1,0:T(8,128)(2,1)S(1)} %collective-permute-done) | copy-start | bytes 786436
  22.6 25.2 %collective-permute-start.1 = (bf16[128,2048]{1,0:T(8,128)(2,1)}, bf16[128,2048]{1,0:T(8,128)(2,1)}, u32[]{:S(2)}, u32[]{:S(2)}) collective-permute-start(bf16[128,2048]{1,0:T(8,128)(2,1)} %pad_maximum_fusion), channel_id=1, source_target_pairs={{0,2},{1,3},{2,0},{3,1},{4,6},{5,7},{6,4},{7,5},{8,10},{9,11},{10,... | collective-permute-start | bytes 1572872 | tf_op jit(solution)/shard_map/ppermute | solution.py:17
  31.9 23.4 %copy-start.20 = (f32[1536]{0:T(1024)S(1)}, f32[1536]{0:T(1024)}, u32[]{:S(2)}) copy-start(f32[1536]{0:T(1024)} %param.32) | copy-start | bytes 18436
  55.3 8.5 %copy-start.8 = (f32[256,256]{0,1:T(8,128)S(1)}, f32[256,256]{0,1:T(8,128)}, u32[]{:S(2)}) copy-start(f32[256,256]{0,1:T(8,128)} %abs_convert_fusion) | copy-start | bytes 786436
  69.3 2.7 copy-start.12
  72.0 1.0 copy-start.1
  73.7 0.8 copy-start.2
  77.6 58.1 %copy-start.6 = (bf16[64,2048]{1,0:T(8,128)(2,1)S(1)}, bf16[64,2048]{1,0:T(8,128)(2,1)}, u32[]{:S(2)}) copy-start(bf16[64,2048]{1,0:T(8,128)(2,1)} %param.28) | copy-start | bytes 786436
  77.7 58.0 %copy-start.15 = (f32[2048]{0:T(1024)S(1)}, f32[2048]{0:T(1024)}, u32[]{:S(2)}) copy-start(f32[2048]{0:T(1024)} %param.36) | copy-start | bytes 24580
  77.7 59.9 %copy-start.16 = (f32[2048]{0:T(1024)S(1)}, f32[2048]{0:T(1024)}, u32[]{:S(2)}) copy-start(f32[2048]{0:T(1024)} %param.38) | copy-start | bytes 24580
  77.7 59.9 %copy-start.17 = (f32[2048]{0:T(1024)S(1)}, f32[2048]{0:T(1024)}, u32[]{:S(2)}) copy-start(f32[2048]{0:T(1024)} %param.37) | copy-start | bytes 24580
  79.5 59.1 %copy-start.19 = (s32[256]{0:T(256)S(1)}, s32[256]{0:T(256)}, u32[]{:S(2)}) copy-start(s32[256]{0:T(256)} %param.48) | copy-start | bytes 3076
  79.5 86.4 %all-gather.4.cloned.1.call-start = ((), (), s32[]{:S(2)}) async-start(), calls=%async_computation.4 | async-start | bytes 1310720 | tf_op jit(solution)/shard_map/all_gather | solution.py:179
  136.8 0.7 copy-start.5
  138.4 64.7 %reduce-scatter.2.cloned.1.call-start = ((), (), s32[]{:S(2)}) async-start(), calls=%async_computation.2 | async-start | bytes 2359296 | tf_op jit(solution)/shard_map/reduce_scatter | solution.py:190
  163.3 2.6 copy-start.21
  163.3 44.4 %copy-start.23 = (s32[64]{0:T(128)S(1)}, s32[64]{0:T(128)}, u32[]{:S(2)}) copy-start(s32[64]{0:T(128)} %param.47) | copy-start | bytes 772
  163.3 67.7 %all-reduce.7.cloned.1.call-start = ((), (), s32[]{:S(2)}) async-start(), calls=%async_computation.5 | async-start | bytes 2097152 | tf_op jit(solution)/shard_map/psum | solution.py:157
  173.6 57.5 %copy-start.18 = (f32[2048]{0:T(1024)S(1)}, f32[2048]{0:T(1024)}, u32[]{:S(2)}) copy-start(f32[2048]{0:T(1024)} %param.42) | copy-start | bytes 24580
  173.6 59.1 %copy-start.13 = (f32[2048]{0:T(1024)S(1)}, f32[2048]{0:T(1024)}, u32[]{:S(2)}) copy-start(f32[2048]{0:T(1024)} %param.30) | copy-start | bytes 24580
  173.6 59.1 %copy-start.14 = (f32[2048]{0:T(1024)S(1)}, f32[2048]{0:T(1024)}, u32[]{:S(2)}) copy-start(f32[2048]{0:T(1024)} %param.29) | copy-start | bytes 24580
  203.1 21.0 %all-to-all-start = ((bf16[4,64,512]{2,1,0:T(8,128)(2,1)}), bf16[4,64,512]{2,1,0:T(8,128)(2,1)S(1)}, u32[]{:S(2)}, u32[]{:S(2)}) async-start(bf16[4,64,512]{2,1,0:T(8,128)(2,1)} %bitcast.134), calls=%async_computation.1 | async-start | bytes 524288 | tf_op jit(solution)/shard_map/all_to_all | solution.py:196
  207.7 146.3 %all-reduce.9.cloned.1.call-start = ((), (), s32[]{:S(2)}) async-start(), calls=%async_computation.6 | async-start | bytes 2097152 | tf_op jit(solution)/shard_map/psum | solution.py:157
  232.9 8.3 %copy-start.7 = (bf16[64,2048]{1,0:T(8,128)(2,1)}, bf16[64,2048]{1,0:T(8,128)(2,1)S(1)}, u32[]{:S(2)}) copy-start(bf16[64,2048]{1,0:T(8,128)(2,1)S(1)} %fusion.67) | copy-start | bytes 786436
  232.9 8.3 %collective-permute-start.2 = (bf16[64,2048]{1,0:T(8,128)(2,1)S(1)}, bf16[64,2048]{1,0:T(8,128)(2,1)S(1)}, u32[]{:S(2)}, u32[]{:S(2)}) collective-permute-start(bf16[64,2048]{1,0:T(8,128)(2,1)S(1)} %fusion.67), channel_id=1, source_target_pairs={{0,3},{1,0},{2,1},{3,2},{4,7},{5,4},{6,5},{7,6},{8,11},{9,8},{10,9... | collective-permute-start | bytes 786440 | tf_op jit(solution)/shard_map/ppermute | solution.py:17
  241.3 0.9 copy-start.10
  242.2 25.5 %collective-permute-start.3 = (bf16[128,2048]{1,0:T(8,128)(2,1)}, bf16[128,2048]{1,0:T(8,128)(2,1)}, u32[]{:S(2)}, u32[]{:S(2)}) collective-permute-start(bf16[128,2048]{1,0:T(8,128)(2,1)} %pad_maximum_fusion.1), channel_id=1, source_target_pairs={{0,2},{1,3},{2,0},{3,1},{4,6},{5,7},{6,4},{7,5},{8,10},{9,11},{10,... | collective-permute-start | bytes 1572872 | tf_op jit(solution)/shard_map/ppermute | solution.py:17
  290.8 2.7 copy-start.11
  293.5 1.0 copy-start.3
  295.2 0.8 copy-start.4
  299.1 84.8 %all-gather.6.cloned.1.call-start = ((), (), s32[]{:S(2)}) async-start(), calls=%async_computation.7 | async-start | bytes 1310720 | tf_op jit(solution)/shard_map/all_gather | solution.py:179
  356.4 86.3 %all-reduce.11.cloned.1.call-start = ((), (), s32[]{:S(2)}) async-start(), calls=%async_computation.8 | async-start | bytes 2097152 | tf_op jit(solution)/shard_map/psum | solution.py:157
Sparse Core Ops, SparseCore 0:
  79.6 56.0 all-reduce.4
  138.6 27.3 all-gather.3
  173.8 57.2 all-reduce.6
  299.2 54.8 all-reduce.8
  356.5 27.3 all-gather.5
  391.4 51.3 all-reduce.10
Sparse Core Ops, SparseCore 1:
  163.4 39.7 reduce-scatter.1
